TPU v7x, 512 devices: a whole 4x8x8 slice. The times are simulated.
512 devices in a mesh: fibre: 64 (over z, x, core), tm: 8 (over y).
Axes of the slice: x: 4, y: 8, z: 8, core: 2. Of those that a mesh axis runs over, the one named last changes fastest.
Arguments:
- traces: bfloat16 [8192, 8192], P('fibre', 'tm'), may hold values from -6 to 6
- stack_weights: bfloat16 [65536, 2048], P('fibre'), may hold values from -0.125 to 0.125
- channel_lists: int32 [64, 64], P('fibre'), may hold values from 0 to 255, as said below
- lag_offsets: int32 [64, 64], P('fibre'), may hold values from 0 to 127
- lengths: int32 [64], P('fibre'), may hold values from 16 to 64, as said below
- class_weights: float32 [256, 4], replicated, may hold values from -0.375 to 0.375
- class_bias: float32 [4], replicated, may hold values from -4 to 4
Outputs:
- log_power: float32 [256, 256], P('fibre')
- logits: float32 [256, 4], P('fibre')
Inputs may be any that keep to these rules, and one draw needn't show every extreme that they name: `channel_lists`: in each row, the values divided by 4 (rounded down) form a permutation of 0 to 63: each region reads exactly one channel block held by each index of fibre. `lengths`: some region has all 64 slots live.
All inputs are finite; a program needn't handle non-finite values.
Results may differ from a plain program's by a relative error of at most 0.0003.
Values may be sent and summed in bfloat16 or wider, within the bound.
A program may use at most 128 MiB of HBM per device.

v0:
```python
import jax
import jax.numpy as jnp
from jax import lax
from jax.sharding import PartitionSpec as P

BLOCK_CH = 32
MAX_LAG = 128
SRC_BLOCK = 256


def passed_along(block, axis, distance):
    devices = range(lax.axis_size(axis))
    route = [(i - distance, i) for i in devices if i - distance in devices]
    return lax.ppermute(block, axis, route)


def lag_tiles(selected, offsets):
    count = selected.shape[0]
    width = selected.shape[2]
    tiles = selected.reshape(count, BLOCK_CH, width // MAX_LAG, MAX_LAG)
    inner = jnp.arange(MAX_LAG, dtype=jnp.int32)
    target = inner[None, None, :] + offsets[:, None, None]
    lower_select = (inner[None, :, None] == target).astype(jnp.bfloat16)
    upper_select = (inner[None, :, None] + MAX_LAG == target).astype(jnp.bfloat16)
    lower = jnp.einsum(
        "scki,sij->sckj", tiles[:, :, :-1], lower_select, preferred_element_type=jnp.float32
    )
    upper = jnp.einsum(
        "scki,sij->sckj", tiles[:, :, 1:], upper_select, preferred_element_type=jnp.float32
    )
    shifted = (lower + upper).astype(jnp.bfloat16)
    return shifted.reshape(count, BLOCK_CH, width - MAX_LAG)


def per_device(
    traces, stack_weights, channel_lists, lag_offsets, lengths, class_weights, class_bias
):
    blocks_here = traces.shape[0] // BLOCK_CH
    segment = traces.shape[1]
    later_rim = passed_along(traces[:, :MAX_LAG], "tm", -1)
    extended = jnp.concatenate([traces, later_rim], axis=1).reshape(
        blocks_here, BLOCK_CH, segment + MAX_LAG
    )
    slot_list = channel_lists[0]
    slot_offsets = lag_offsets[0]
    list_length = slot_list.shape[0]
    slot_range = jnp.arange(list_length, dtype=jnp.int32)
    owners = slot_list // blocks_here
    local_block = slot_list % blocks_here
    live_slots = slot_range < lengths[0]
    matched = owners[:, None] == slot_range[None, :]
    slot_of_owner = jnp.sum(jnp.where(matched, slot_range[:, None], 0), axis=0)
    wanted = jnp.stack(
        [jnp.take(local_block, slot_of_owner), jnp.take(slot_offsets, slot_of_owner)], axis=1
    )
    incoming = lax.all_to_all(wanted, "fibre", split_axis=0, concat_axis=0, tiled=True)
    selected = jnp.take(extended, incoming[:, 0], axis=0)
    outgoing = lag_tiles(selected, incoming[:, 1])
    live_mask = live_slots.astype(jnp.bfloat16)
    received = lax.all_to_all(outgoing, "fibre", split_axis=0, concat_axis=0, tiled=True)
    ordered = jnp.take(received, owners, axis=0) * live_mask[:, None, None]
    flattened = ordered.reshape(list_length * BLOCK_CH, received.shape[2])
    beams = jnp.dot(stack_weights, flattened, preferred_element_type=jnp.float32)
    partial_energy = jnp.sum(beams * beams, axis=1)
    total_energy = lax.psum(partial_energy, "tm")
    beam_power = total_energy / (segment * lax.axis_size("tm"))
    log_power = jnp.log(beam_power + 1e-06).reshape(-1, SRC_BLOCK)
    logits = jnp.dot(log_power, class_weights, precision=lax.Precision.HIGHEST) + class_bias
    return (log_power, logits)


def solution(mesh):
    placed = (
        P("fibre", "tm"),
        P("fibre", None),
        P("fibre", None),
        P("fibre", None),
        P("fibre"),
        P(),
        P(),
    )
    return jax.shard_map(
        per_device,
        mesh=mesh,
        in_specs=placed,
        out_specs=(P("fibre", None), P("fibre", None)),
        check_vma=False,
    )
```

profile of v0, /device:TPU:2, one launch (start us, length us, event | category | flops | bytes accessed | tf_op | source)
XLA Modules:
  0.0 209.4 jit_solution(10583357706433429437)
XLA Ops:
  0.6 0.7 compare_and_fusion.1
  1.3 0.7 and_select_fusion.1
  2.1 0.8 gather_fusion.2
  2.9 1.4 gather_fusion.3
  4.3 0.7 copy.11
  5.0 13.9 %all-to-all-start = ((s32[64,1,2]{2,1,0:T(1,128)}), s32[64,1,2]{2,1,0:T(1,128)S(1)}, u32[]{:S(2)}, u32[]{:S(2)}) async-start(s32[64,1,2]{2,1,0:T(1,128)} %copy.11), calls=%async_computation | async-start | bytes 65536 | tf_op jit(solution)/shard_map/all_to_all | solution.py:56
  18.9 0.8 slice.16
  19.7 1.3 collective-permute-start
  21.0 6.5 %all-to-all-done = s32[64,1,2]{2,1,0:T(1,128)S(1)} async-done(((s32[64,1,2]{2,1,0:T(1,128)}), s32[64,1,2]{2,1,0:T(1,128)S(1)}, u32[]{:S(2)}, u32[]{:S(2)}) %all-to-all-start) | async-done | bytes 544 | tf_op jit(solution)/shard_map/all_to_all | solution.py:56
  27.7 1.0 pad_maximum_fusion
  28.6 3.2 %gather_fusion = bf16[64,32,1152]{2,1,0:T(8,128)(2,1)} fusion(bf16[4,32,1152]{2,1,0:T(8,128)(2,1)S(1)} %bitcast.68, s32[1024]{0:T(1024)S(1)} %pad_clamp_fusion.1), kind=kCustom, calls=%fused_computation.2 | custom fusion | bytes 9437440 | tf_op jit(solution)/shard_map/jit(_take)/gather | solution.py:57
  31.8 10.5 %gather.16 = bf16[64,32,9,128]{3,2,1,0:T(8,128)(2,1)} reshape(bf16[64,32,1152]{2,1,0:T(8,128)(2,1)} %gather_fusion) | data formatting | bytes 9437184 | tf_op jit(solution)/shard_map/jit(_take)/gather | solution.py:57
  42.3 7.5 %broadcast_select_fusion = bf16[64,32,9,128]{3,2,1,0:T(8,128)(2,1)} fusion(bf16[64,32,9,128]{3,2,1,0:T(8,128)(2,1)} %gather.16, pred[64]{0:T(512)(128)(4,1)S(1)} %and_bitcast_fusion), kind=kLoop, calls=%fused_computation.5 | loop fusion | flops 2359296 | bytes 9437248 | tf_op jit(solution)/shard_map/jit(_take)/select_n | solution.py:57
  49.8 6.7 %fusion.2 = f32[64,32,8,128]{3,2,1,0:T(8,128)} fusion(bf16[64,32,9,128]{3,2,1,0:T(8,128)(2,1)} %broadcast_select_fusion, s32[64,128]{1,0:T(8,128)S(1)} %iota_add_fusion), kind=kOutput, calls=%fused_computation.8 | convolution fusion | flops 537919488 | bytes 12615680 | tf_op jit(solution)/shard_map/scki,sij->sckj/dot_general | solution.py:25
  56.4 10.1 %add_convert_fusion = bf16[64,32,8,128]{3,2,1,0:T(8,128)(2,1)} fusion(f32[64,32,8,128]{3,2,1,0:T(8,128)} %fusion.2, bf16[64,32,9,128]{3,2,1,0:T(8,128)(2,1)} %broadcast_select_fusion, s32[64,128]{1,0:T(8,128)S(1)} %iota_add_fusion, s32[128]{0:T(128)S(1)} %iota_add_fusion.1), kind=kOutput, calls=%fused_computation.4 | convolution fusion | flops 542113792 | bytes 16810496 | tf_op jit(solution)/shard_map/scki,sij->sckj/dot_general | solution.py:28
  66.5 7.3 %reshape.159 = bf16[64,32,1024]{2,1,0:T(8,128)(2,1)} reshape(bf16[64,32,8,128]{3,2,1,0:T(8,128)(2,1)} %add_convert_fusion) | data formatting | bytes 8388608 | tf_op jit(solution)/shard_map/reshape | solution.py:32
  73.8 8.4 %all-to-all-start.1 = ((bf16[64,32,1024]{2,1,0:T(8,128)(2,1)}), bf16[64,32,1024]{2,1,0:T(8,128)(2,1)}, u32[]{:S(2)}, u32[]{:S(2)}) async-start(bf16[64,32,1024]{2,1,0:T(8,128)(2,1)} %reshape.159), calls=%async_computation.1 | async-start | bytes 8388608 | tf_op jit(solution)/shard_map/all_to_all | solution.py:60
  83.3 95.1 %all-to-all-done.1 = bf16[64,32,1024]{2,1,0:T(8,128)(2,1)} async-done(((bf16[64,32,1024]{2,1,0:T(8,128)(2,1)}), bf16[64,32,1024]{2,1,0:T(8,128)(2,1)}, u32[]{:S(2)}, u32[]{:S(2)}) %all-to-all-start.1) | async-done | bytes 4194336 | tf_op jit(solution)/shard_map/all_to_all | solution.py:60
  178.4 5.0 %gather_fusion.1 = bf16[64,32,1024]{2,1,0:T(8,128)(2,1)} fusion(bf16[64,32,1024]{2,1,0:T(8,128)(2,1)} %all-to-all-done.1, s32[1024]{0:T(1024)S(1)} %pad_clamp_fusion), kind=kCustom, calls=%fused_computation.3 | custom fusion | bytes 8388864 | tf_op jit(solution)/shard_map/jit(_take)/gather | solution.py:61
  183.3 2.7 %fusion.4 = bf16[2048,1024]{1,0:T(8,128)(2,1)S(1)} fusion(bf16[64,32,1024]{2,1,0:T(8,128)(2,1)} %gather_fusion.1, pred[2048]{0:T(1024)(128)(4,1)S(1)} %broadcast_in_dim.51, bf16[2048]{0:T(1024)(128)(2,1)S(1)} %mul.18), kind=kLoop, calls=%fused_computation.11 | loop fusion | flops 4194304 | bytes 8394752 | tf_op jit(solution)/shard_map/mul | solution.py:61
  186.1 0.7 copy-done.3
  186.8 4.8 %multiply_reduce_fusion = f32[1024]{0:T(1024)S(1)} fusion(bf16[2048,1024]{1,0:T(8,128)(2,1)S(1)} %fusion.4, bf16[1024,2048]{1,0:T(8,128)(2,1)S(1)} %copy-done.3), kind=kOutput, calls=%fused_computation.12 | convolution fusion | flops 4297063424 | bytes 8392704 | tf_op jit(solution)/shard_map/dot_general | solution.py:63
  191.6 17.1 %psum.7 = f32[1024]{0:T(1024)S(1)} all-reduce(f32[1024]{0:T(1024)S(1)} %multiply_reduce_fusion), channel_id=1, replica_groups=mesh['fibre'=64,'tm'=8] {'tm'}, use_global_device_ids=true, to_apply=%region_2.4 | all-reduce | flops 1024 | bytes 8192 | tf_op jit(solution)/shard_map/psum | solution.py:65
  208.7 0.7 convolution_add_fusion
  (30 shorter events, 0.7 us)
Async XLA Ops:
  0.6 208.0 %copy-start = (f32[256,4]{0,1:T(4,128)S(1)}, f32[256,4]{0,1:T(4,128)}, u32[]{:S(2)}) copy-start(f32[256,4]{0,1:T(4,128)} %param.14) | copy-start | bytes 12292
  5.0 22.4 %all-to-all-start = ((s32[64,1,2]{2,1,0:T(1,128)}), s32[64,1,2]{2,1,0:T(1,128)S(1)}, u32[]{:S(2)}, u32[]{:S(2)}) async-start(s32[64,1,2]{2,1,0:T(1,128)} %copy.11), calls=%async_computation | async-start | bytes 65536 | tf_op jit(solution)/shard_map/all_to_all | solution.py:56
  19.7 8.0 %collective-permute-start = (bf16[128,128]{1,0:T(8,128)(2,1)S(1)}, bf16[128,128]{1,0:T(8,128)(2,1)S(1)}, u32[]{:S(2)}, u32[]{:S(2)}) collective-permute-start(bf16[128,128]{1,0:T(8,128)(2,1)S(1)} %slice.16), channel_id=1, source_target_pairs={{1,0},{2,1},{3,2},{4,3},{5,4},{6,5},{7,6},{9,8},{10,9},{11,10},{12... | collective-permute-start | bytes 98312 | tf_op jit(solution)/shard_map/ppermute | solution.py:14
  73.8 9.4 %copy-start.4 = (s32[1,64]{1,0:T(1,128)S(1)}, s32[1,64]{1,0:T(1,128)}, u32[]{:S(2)}) copy-start(s32[1,64]{1,0:T(1,128)} %param.11) | copy-start | bytes 772
  73.8 104.5 %all-to-all-start.1 = ((bf16[64,32,1024]{2,1,0:T(8,128)(2,1)}), bf16[64,32,1024]{2,1,0:T(8,128)(2,1)}, u32[]{:S(2)}, u32[]{:S(2)}) async-start(bf16[64,32,1024]{2,1,0:T(8,128)(2,1)} %reshape.159), calls=%async_computation.1 | async-start | bytes 8388608 | tf_op jit(solution)/shard_map/all_to_all | solution.py:60
  183.3 3.4 %copy-start.3 = (bf16[1024,2048]{1,0:T(8,128)(2,1)S(1)}, bf16[1024,2048]{1,0:T(8,128)(2,1)}, u32[]{:S(2)}) copy-start(bf16[1024,2048]{1,0:T(8,128)(2,1)} %param.10) | copy-start | bytes 12582916
  186.8 21.9 %copy-start.2 = (f32[4]{0:T(128)S(1)}, f32[4]{0:T(128)}, u32[]{:S(2)}) copy-start(f32[4]{0:T(128)} %param.15) | copy-start | bytes 52
  208.7 0.7 copy-start.1
where the time goes:
time: 210 us; the launch traced here: 209 us
  waiting for transfers between devices  102 us (49%)
  local copies, waits for them, and re-layouts  30.8 us (15%)
  starting transfers between devices  23.6 us (11%)
  matrix products  22.2 us (11%)
  blocking collectives  17.1 us (8%)
  other arithmetic  12.8 us (6%)
    all_to_all x1, waiting for transfers between devices, per_device(): lax.all_to_all(outgoing, 'fibre', split_axis=0, concat_axis=0, tiled=True)  95.1 us
    psum x1, blocking collectives, per_device(): total_energy = lax.psum(partial_energy, 'tm')  17.1 us
    all_to_all x1, starting transfers between devices, per_device(): lax.all_to_all(wanted, 'fibre', split_axis=0, concat_axis=0, tiled=True)  13.9 us
    gather x2, local copies, waits for them, and re-layouts, per_device(): selected = jnp.take(extended, incoming[:, 0], axis=0)  13.6 us
    dot_general x1, matrix products, lag_tiles(): jnp.einsum('scki,sij->sckj', tiles[:, :, 1:], upper_select, preferred_ele...  10.1 us
    all_to_all x1, starting transfers between devices, per_device(): lax.all_to_all(outgoing, 'fibre', split_axis=0, concat_axis=0, tiled=True)  8.42 us
    select_n x1, other arithmetic, per_device(): selected = jnp.take(extended, incoming[:, 0], axis=0)  7.47 us
    reshape x1, local copies, waits for them, and re-layouts, lag_tiles(): return shifted.reshape(count, BLOCK_CH, width - MAX_LAG)  7.33 us
  transfers between devices with their start and end apart: 3, of which 2 were waited for; matrix products, arithmetic and copies ran while one was open for 1% of the time, Pallas kernels for 0%

commit v1 on v0

v1 whole, which is shorter than its diff:
```python
import functools

import jax
import jax.numpy as jnp
from jax import lax
from jax.experimental import pallas as pl
from jax.experimental.pallas import tpu as pltpu
from jax.sharding import PartitionSpec as P

BLOCK_CH = 32
MAX_LAG = 128
SRC_BLOCK = 256
NX = 4
MESH = pl.DeviceIdType.MESH


def kernel(nz, ny, samples, tab_ref, key_ref, traces_ref, w_ref, cw_ref, cb_ref, lp_ref, lg_ref, *scratch):
    nf = nz // 2
    nb = nz - 1 - nf
    labels = [("o", 0)]
    for h in range(1, nf + 1):
        labels.append(("f", h))
        if h <= nb:
            labels.append(("b", h))
    at = {label: i for i, label in enumerate(labels)}
    gz = scratch[:nz]
    gx = scratch[nz : 2 * nz]
    (
        tiles, stage, w_v, perm_v, wp_v, acc, tabs_v, tabs_s, ebuf,
        loc_sem, halo_sem, tab_send, tab_recv, smem_sem,
        z_send, z_recv, x_send, x_recv, t_send, t_recv, y_send, y_recv,
    ) = scratch[2 * nz :]
    seg = traces_ref.shape[2]
    rows = w_ref.shape[0]
    depth = w_ref.shape[1]
    chunk = 2 * NX * BLOCK_CH

    me = lax.axis_index("fibre")
    y = lax.axis_index("tm")
    c = lax.rem(me, 2)
    x = lax.rem(me // 2, NX)
    z = me // (2 * NX)
    d = 1 - 2 * c
    e = 1 - c

    def dev(zz, xx, cc):
        return {"fibre": (lax.rem(zz + 2 * nz, nz) * NX + lax.rem(xx + 2 * NX, NX)) * 2 + cc}

    def zoff(label):
        kind, h = label
        return {"o": 0, "f": -d * h, "b": d * h}[kind]

    def tslot(label):
        return lax.rem(zoff(label) + nz, nz)

    def col(xx, cc):
        return lax.rem(xx + 2 * NX, NX) * 2 + cc

    sibling = dev(z, x, e)
    fore, back = dev(z, x + d, c), dev(z, x - d, c)
    fore_e, back_e = dev(z, x + d, e), dev(z, x - d, e)
    zfore, zback = dev(z + d, x, c), dev(z - d, x, c)
    peers = [sibling, fore, back, fore_e, back_e]
    ring = [zfore, zback] if nb else [zfore]
    others = [{"tm": lax.rem(y + k, ny)} for k in range(1, ny)]

    barrier = pltpu.get_barrier_semaphore()
    for peer in peers + ring + others:
        pl.semaphore_signal(barrier, inc=1, device_id=peer, device_id_type=MESH)
    pl.semaphore_wait(barrier, len(peers) + len(ring) + len(others))

    def remote(src, dst, ssem, rsem, device):
        return pltpu.make_async_remote_copy(
            src_ref=src, dst_ref=dst, send_sem=ssem, recv_sem=rsem, device_id=device, device_id_type=MESH
        )

    own = gz[0]
    halo = remote(
        traces_ref.at[:, :, pl.ds(0, MAX_LAG)], own.at[:, :, pl.ds(seg, MAX_LAG)],
        halo_sem.at[0], halo_sem.at[1], {"tm": lax.rem(y + ny - 1, ny)},
    )
    if ny > 1:
        @pl.when(y > 0)
        def _():
            halo.start()
    own_copy = pltpu.make_async_copy(traces_ref, own.at[:, :, pl.ds(0, seg)], loc_sem.at[0])
    own_copy.start()
    slots = [1, 2, 4, 5, 3]
    tab_copies = [
        remote(tab_ref, tabs_v.at[slot], tab_send.at[i], tab_recv.at[slot], peer)
        for i, (slot, peer) in enumerate(zip(slots, peers))
    ]
    for copy in tab_copies:
        copy.start()
    w_copy = pltpu.make_async_copy(w_ref, w_v, loc_sem.at[1])
    w_copy.start()
    tabs_v[0] = tab_ref[...]

    @pl.when(y == ny - 1)
    def _():
        own[:, :, seg:] = jnp.zeros((own.shape[0], BLOCK_CH, MAX_LAG), jnp.bfloat16)

    own_copy.wait()
    if ny > 1:
        @pl.when(y < ny - 1)
        def _():
            halo.wait_recv()

    sent = []

    def start(copy):
        copy.start()
        sent.append(copy)

    def pass_along(label):
        kind, h = label
        i = at[label]
        if kind in "of" and h < nf:
            n = at[("f", h + 1)]
            start(remote(gz[i], gz[n], z_send.at[n], z_recv.at[n], zfore))
        if kind in "ob" and h < nb:
            n = at[("b", h + 1)]
            start(remote(gz[i], gz[n], z_send.at[n], z_recv.at[n], zback))
        start(remote(gz[i], gx[i], x_send.at[i], x_recv.at[i], fore))

    lane = lax.broadcasted_iota(jnp.int32, (BLOCK_CH, MAX_LAG), 1)

    def cut(src, region, owner, dst):
        word = tabs_s[region, 0, owner]
        block = lax.bitwise_and(word, 3)
        lag = lax.shift_right_logical(word, 2)
        turn = lax.bitwise_and(MAX_LAG - lag, MAX_LAG - 1)
        near = lane < MAX_LAG - lag
        held = pltpu.roll(src[block, :, 0:MAX_LAG].astype(jnp.float32), turn, 1)
        for j in range(seg // MAX_LAG):
            following = pltpu.roll(
                src[block, :, (j + 1) * MAX_LAG : (j + 2) * MAX_LAG].astype(jnp.float32), turn, 1
            )
            dst[:, j * MAX_LAG : (j + 1) * MAX_LAG] = jnp.where(near, held, following).astype(jnp.bfloat16)
            held = following

    def deal(src, label, xo, regions, base):
        t = tslot(label)
        owner = lax.rem(z + zoff(label) + nz, nz) * 2 * NX + col(xo, c)
        k = col(xo, c)
        for j, (region, peer) in enumerate(regions):
            n = base + j
            cut(src, region, owner, stage.at[n])
            start(remote(stage.at[n], tiles.at[t, k], t_send.at[n], t_recv.at[t, k], peer))
        cut(src, 0, owner, tiles.at[t, k])

    def near_tiles(label):
        deal(gz[at[label]], label, x, [(2, back), (3, back_e), (1, sibling)], 6 * at[label])

    def far_tiles(label):
        deal(gx[at[label]], label, x - d, [(4, fore), (5, fore_e), (1, sibling)], 6 * at[label] + 3)

    def wait_z(label):
        i = at[label]
        remote(gz[i], gz[i], z_send.at[i], z_recv.at[i], zfore).wait_recv()

    def wait_x(label):
        i = at[label]
        remote(gx[i], gx[i], x_send.at[i], x_recv.at[i], fore).wait_recv()

    def wait_tiles(label):
        t = tslot(label)
        ks = [col(x + d, c), col(x + 2, c), col(x, e), col(x + d, e), col(x - d, e), col(x + 2, e)]
        for k in ks:
            remote(stage.at[0], tiles.at[t, k], t_send.at[0], t_recv.at[t, k], fore).wait_recv()

    def arrange(label):
        i = at[label]
        first = lax.rem(z + zoff(label) + nz, nz) * chunk
        for kk in range(depth // chunk):
            wanted = lax.broadcasted_iota(jnp.int32, (chunk, chunk), 0) + first
            hit = key_ref[0:1, kk * chunk : (kk + 1) * chunk] == wanted
            perm_v[:, kk * chunk : (kk + 1) * chunk] = jnp.where(hit, 1.0, 0.0).astype(jnp.bfloat16)
        step = min(rows, 256)

        def body(r, carry):
            at_row = pl.multiple_of(r * step, step)
            wp_v[i, pl.ds(at_row, step), :] = lax.dot_general(
                w_v[pl.ds(at_row, step), :], perm_v[...], (((1,), (1,)), ((), ())),
                preferred_element_type=jnp.float32,
            ).astype(jnp.bfloat16)
            return carry

        lax.fori_loop(0, rows // step, body, 0)

    width = min(seg, 256)

    def add_chunk(label, first):
        t = tslot(label)
        i = at[label]

        def body(n, carry):
            cols = pl.ds(pl.multiple_of(n * width, width), width)
            part = jnp.dot(
                wp_v[i], tiles[t, :, :, cols].reshape(chunk, width), preferred_element_type=jnp.float32
            )
            acc[n] = part if first else acc[n] + part
            return carry

        lax.fori_loop(0, seg // width, body, 0)

    pass_along(labels[0])
    for slot, peer in zip(slots, peers):
        remote(tab_ref, tabs_v.at[slot], tab_send.at[0], tab_recv.at[slot], peer).wait_recv()
    to_smem = pltpu.make_async_copy(tabs_v, tabs_s, smem_sem)
    to_smem.start()
    to_smem.wait()
    near_tiles(labels[0])
    w_copy.wait()

    z_queue = list(labels[1:])
    x_queue = list(labels)
    chunks_left = list(labels)
    arrange_left = list(labels)
    done_x = []

    def step_z():
        label = z_queue.pop(0)
        wait_z(label)
        pass_along(label)
        near_tiles(label)

    def step_x():
        label = x_queue.pop(0)
        wait_x(label)
        far_tiles(label)
        done_x.append(label)

    def step_chunk():
        label = chunks_left.pop(0)
        wait_tiles(label)
        add_chunk(label, label == labels[0])

    while z_queue or x_queue:
        if arrange_left:
            arrange(arrange_left.pop(0))
        if z_queue:
            step_z()
        if z_queue:
            step_z()
        if x_queue:
            step_x()
        if len(done_x) > 1 and len(chunks_left) > len(labels) - len(done_x) + 1:
            step_chunk()
    while arrange_left:
        arrange(arrange_left.pop(0))
    while chunks_left:
        step_chunk()

    block = 128
    for r in range(rows // block):
        total = jnp.zeros((block, 128), jnp.float32)
        for n in range(seg // width):
            for j in range(width // 128):
                part = acc[n, r * block : (r + 1) * block, j * 128 : (j + 1) * 128]
                total = total + part * part
        ebuf[y, r : r + 1, :] = jnp.sum(total.T, axis=0, keepdims=True)

    for k, peer in enumerate(others):
        start(remote(ebuf.at[y], ebuf.at[y], y_send.at[k], y_recv.at[y], peer))
    for k in range(1, ny):
        source = lax.rem(y + k, ny)
        remote(ebuf.at[source], ebuf.at[source], y_send.at[0], y_recv.at[source], others[0]).wait_recv()
    energy = ebuf[0]
    for k in range(1, ny):
        energy = energy + ebuf[k]
    log_power = jnp.log(energy / samples + 1e-06)
    per = SRC_BLOCK // block
    for r in range(rows // block):
        lp_ref[r // per : r // per + 1, (r % per) * block : (r % per + 1) * block] = log_power[r : r + 1, :]
    lg_ref[...] = (
        jnp.dot(lp_ref[...], cw_ref[...], precision=lax.Precision.HIGHEST, preferred_element_type=jnp.float32)
        + cb_ref[...]
    )
    for copy in sent:
        copy.wait_send()
    for copy in tab_copies:
        copy.wait_send()
    if ny > 1:
        @pl.when(y > 0)
        def _():
            halo.wait_send()


def per_device(nz, ny, traces, stack_weights, channel_lists, lag_offsets, lengths, class_weights, class_bias):
    blocks = traces.shape[0] // BLOCK_CH
    seg = traces.shape[1]
    rows, depth = stack_weights.shape
    count = channel_lists.shape[1]
    chunk = 2 * NX * BLOCK_CH
    owners = channel_lists[0] // blocks
    slot = jnp.arange(count, dtype=jnp.int32)
    word = channel_lists[0] % blocks + 4 * lag_offsets[0]
    table = jnp.sum(jnp.where(owners[:, None] == jnp.arange(128, dtype=jnp.int32)[None, :], word[:, None], 0), axis=0)
    table = jnp.broadcast_to(table[None, :], (8, 128))
    keyed = jnp.where(
        (slot < lengths[0])[:, None], owners[:, None] * BLOCK_CH + jnp.arange(BLOCK_CH, dtype=jnp.int32)[None, :], -1
    )
    key = jnp.broadcast_to(keyed.reshape(1, depth), (8, depth))
    bf16, f32 = jnp.bfloat16, jnp.float32
    vmem = pl.BlockSpec(memory_space=pltpu.VMEM)
    hbm = pl.BlockSpec(memory_space=pl.ANY)
    dma = pltpu.SemaphoreType.DMA
    width = min(seg, 256)
    scratch = [pltpu.VMEM((blocks, BLOCK_CH, seg + MAX_LAG), bf16) for _ in range(2 * nz)] + [
        pltpu.VMEM((nz, 2 * NX, BLOCK_CH, seg), bf16),
        pltpu.VMEM((6 * nz, BLOCK_CH, seg), bf16),
        pltpu.VMEM((rows, depth), bf16),
        pltpu.VMEM((chunk, depth), bf16),
        pltpu.VMEM((nz, rows, chunk), bf16),
        pltpu.VMEM((seg // width, rows, width), f32),
        pltpu.VMEM((6, 8, 128), jnp.int32),
        pltpu.SMEM((6, 8, 128), jnp.int32),
        pltpu.VMEM((ny, rows // 128, 128), f32),
        dma((2,)), dma((2,)), dma((5,)), dma((6,)), dma,
        dma((nz,)), dma((nz,)), dma((nz,)), dma((nz,)), dma((6 * nz,)), dma((nz, 2 * NX)), dma((ny,)), dma((ny,)),
    ]
    return pl.pallas_call(
        functools.partial(kernel, nz, ny, float(seg * ny)),
        out_shape=(
            jax.ShapeDtypeStruct((rows // SRC_BLOCK, SRC_BLOCK), f32),
            jax.ShapeDtypeStruct((rows // SRC_BLOCK, class_weights.shape[1]), f32),
        ),
        in_specs=[vmem, vmem, hbm, hbm, vmem, vmem],
        out_specs=(vmem, vmem),
        scratch_shapes=scratch,
        compiler_params=pltpu.CompilerParams(
            collective_id=0, has_side_effects=True, vmem_limit_bytes=56 * 1024 * 1024
        ),
    )(table, key, traces.reshape(blocks, BLOCK_CH, seg), stack_weights, class_weights, class_bias.reshape(1, -1))


def solution(mesh):
    placed = (
        P("fibre", "tm"),
        P("fibre", None),
        P("fibre", None),
        P("fibre", None),
        P("fibre"),
        P(),
        P(),
    )
    nz = mesh.shape["fibre"] // (2 * NX)
    return jax.shard_map(
        functools.partial(per_device, nz, mesh.shape["tm"]),
        mesh=mesh,
        in_specs=placed,
        out_specs=(P("fibre", None), P("fibre", None)),
        check_vma=False,
    )
```

time: 210 us -> 104 us (0.50)
  the two profiles are of different devices: /device:TPU:2 before, /device:TPU:1 now
where the time goes in v1:
time: 104 us
  Pallas kernels  96.7 us (93%)
  local copies, waits for them, and re-layouts  5.26 us (5%)
  between operations  1.3 us (1%)
    pallas_call x1, Pallas kernels, per_device(): pl.pallas_call(functools.partial(kernel, nz, ny, float(seg * ny)), out_sh...  96.7 us
    unnamed x3, local copies, waits for them, and re-layouts  3.96 us

profile of v1, /device:TPU:1, one launch (start us, length us, event | category | flops | bytes accessed | tf_op | source)
XLA Modules:
  0.0 104.1 jit_solution(4931482906627626143)
XLA Ops:
  1.3 0.7 broadcast_multiply_fusion
  2.0 0.1 select_reduce_fusion
  2.1 0.6 broadcast_in_dim.43.tab_ref
  2.7 0.1 add_select_fusion
  2.8 0.1 select_n.42
  2.8 0.6 broadcast_in_dim.46.key_ref
  3.5 1.5 %copy.11.cw_ref = f32[256,4]{1,0:T(8,128)} copy(f32[256,4]{0,1:T(4,128)} %param.12) | data formatting | bytes 8192 | tf_op args[5]
  4.9 96.7 %shard_map.86 = (f32[4,256]{1,0:T(4,128)}, f32[4,4]{1,0:T(4,128)}) custom-call(s32[8,128]{1,0:T(8,128)} %broadcast_in_dim.43.tab_ref, s32[8,2048]{1,0:T(8,128)} %broadcast_in_dim.46.key_ref, bf16[4,32,1024]{2,1,0:T(8,128)(2,1)} %bitcast.22, bf16[1024,2048]{1,0:T(8,128)(2,1)} %w_ref.1, f32[256,4]{1,0:T(8,128)} %copy.11.cw_ref, f32[1,4]{1,0:T(1,128)} %bitcast.23), custom_call_target="tpu_custom_call" | custom-call | tf_op jit(solution)/shard_map/pallas_call | solution.py:323
  101.6 1.3 %copy.15 = f32[4,256]{1,0:T(4,128)} copy(f32[4,256]{1,0:T(4,128)} %get-tuple-element.7) | data formatting | bytes 8192
  102.9 1.2 %copy.16 = f32[4,4]{1,0:T(4,128)} copy(f32[4,4]{1,0:T(4,128)} %get-tuple-element.8) | data formatting | bytes 128
  (1 shorter events, 0.0 us)

commit v2 on v1

v2 whole, which is shorter than its diff:
```python
import functools

import jax
import jax.numpy as jnp
from jax import lax
from jax.experimental import pallas as pl
from jax.experimental.pallas import tpu as pltpu
from jax.sharding import PartitionSpec as P

BLOCK_CH = 32
MAX_LAG = 128
SRC_BLOCK = 256
NX = 4
HALF = BLOCK_CH // 2
MESH = pl.DeviceIdType.MESH


def kernel(
    nz, ny, samples, list_ref, lag_ref, len_ref, traces_ref, w_ref, cw_ref, cb_ref, lp_ref, lg_ref, *scratch
):
    nf = nz // 2
    nb = nz - 1 - nf
    labels = [("o", 0)]
    for h in range(1, nf + 1):
        labels.append(("f", h))
        if h <= nb:
            labels.append(("b", h))
    at = {label: i for i, label in enumerate(labels)}
    gz = scratch[:nz]
    gx = scratch[nz : 2 * nz]
    (
        tiles, full, half, w_v, perm_v, wp_v, acc, pad, tab_v, tabs_v, tabs_s, ebuf,
        loc_sem, halo_sem, tab_send, tab_recv, smem_sem,
        z_send, z_recv, x_send, x_recv, f_send, h_send, t_recv, y_send, y_recv,
    ) = scratch[2 * nz :]
    seg = traces_ref.shape[2]
    rows = w_ref.shape[0]
    depth = w_ref.shape[1]
    count = list_ref.shape[1]
    chunk = 2 * NX * BLOCK_CH

    me = lax.axis_index("fibre")
    y = lax.axis_index("tm")
    c = lax.rem(me, 2)
    x = lax.rem(me // 2, NX)
    z = me // (2 * NX)
    d = 1 - 2 * c
    e = 1 - c

    def dev(zz, xx, cc):
        return {"fibre": (lax.rem(zz + 2 * nz, nz) * NX + lax.rem(xx + 2 * NX, NX)) * 2 + cc}

    def zoff(label):
        kind, h = label
        return {"o": 0, "f": -d * h, "b": d * h}[kind]

    def tslot(label):
        return lax.rem(zoff(label) + nz, nz)

    def col(xx, cc):
        return lax.rem(xx + 2 * NX, NX) * 2 + cc

    sibling = dev(z, x, e)
    peers = [sibling] + [dev(z, x + s, cc) for s in (1, -1, 2) for cc in (c, e)]
    slots = [1, 4, 5, 2, 3, 6, 7]
    opposite = peers[5]
    zfore, zback = dev(z + d, x, c), dev(z - d, x, c)
    ring = [zfore, zback] if nb else [zfore]
    others = [{"tm": lax.rem(y + k, ny)} for k in range(1, ny)]

    barrier = pltpu.get_barrier_semaphore()
    for peer in peers + ring + others:
        pl.semaphore_signal(barrier, inc=1, device_id=peer, device_id_type=MESH)
    pl.semaphore_wait(barrier, len(peers) + len(ring) + len(others))

    def remote(src, dst, ssem, rsem, device):
        return pltpu.make_async_remote_copy(
            src_ref=src, dst_ref=dst, send_sem=ssem, recv_sem=rsem, device_id=device, device_id_type=MESH
        )

    sent = []

    def start(copy):
        copy.start()
        sent.append(copy)

    own = gz[0]
    hi = pl.ds(HALF, HALF)
    main, rim = pl.ds(0, seg), pl.ds(seg, MAX_LAG)
    halo = remote(
        traces_ref.at[:, :, pl.ds(0, MAX_LAG)], own.at[:, :, rim],
        halo_sem.at[0], halo_sem.at[1], {"tm": lax.rem(y + ny - 1, ny)},
    )
    if ny > 1:
        @pl.when(y > 0)
        def _():
            halo.start()
    firsts = [(at[("f", 1)], zfore)] + ([(at[("b", 1)], zback)] if nb else [])
    for n, peer in firsts:
        start(remote(traces_ref, gz[n].at[:, :, main], z_send.at[n, 0], z_recv.at[n, 0], peer))
    start(remote(traces_ref.at[:, hi], gx[0].at[:, :, main], x_send.at[0, 0], x_recv.at[0, 0], opposite))
    own_copy = pltpu.make_async_copy(traces_ref, own.at[:, :, main], loc_sem.at[0])
    own_copy.start()
    w_copy = pltpu.make_async_copy(w_ref, w_v, loc_sem.at[1])
    w_copy.start()

    @pl.when(y == ny - 1)
    def _():
        own[:, :, seg:] = jnp.zeros((own.shape[0], BLOCK_CH, MAX_LAG), jnp.bfloat16)

    pad[...] = jnp.zeros_like(pad)
    pad[0:1, 0:count] = list_ref[...] + 256 * lag_ref[...]
    asked = jnp.broadcast_to(pad[0:1, :], (128, 128)).T[0:count, :]
    owner_of = lax.shift_right_logical(lax.bitwise_and(asked, 255), 2)
    word = lax.bitwise_or(
        lax.bitwise_and(asked, 3), lax.shift_left(lax.shift_right_logical(asked, 8), 2)
    )
    wanted = lax.broadcasted_iota(jnp.int32, (count, 128), 1)
    table = jnp.sum(jnp.where(owner_of == wanted, word, 0), axis=0, keepdims=True)
    tab_v[...] = jnp.broadcast_to(table, (8, 128))
    tabs_v[0] = tab_v[...]
    for i, (slot, peer) in enumerate(zip(slots, peers)):
        start(remote(tab_v, tabs_v.at[slot], tab_send.at[i], tab_recv.at[slot], peer))

    live = lax.broadcasted_iota(jnp.int32, (1, count), 1) < len_ref[...]
    keyed = jnp.where(live, lax.shift_right_logical(list_ref[...], 2), 2 * nz * NX)
    spread = lax.shift_right_logical(lax.broadcasted_iota(jnp.int32, (count, depth), 1), 5)
    spread = spread == lax.broadcasted_iota(jnp.int32, (count, depth), 0)
    key = jnp.dot(
        jnp.broadcast_to(keyed, (8, count)).astype(jnp.float32).astype(jnp.bfloat16),
        jnp.where(spread, 1.0, 0.0).astype(jnp.bfloat16),
        preferred_element_type=jnp.float32,
    )
    inner = lax.bitwise_and(lax.broadcasted_iota(jnp.int32, (1, depth), 1), BLOCK_CH - 1)
    key = key[0:1, :].astype(jnp.int32) * BLOCK_CH + inner

    def arrange(label):
        i = at[label]
        first = lax.rem(z + zoff(label) + nz, nz) * chunk
        target = lax.broadcasted_iota(jnp.int32, (chunk, chunk), 0) + first
        for kk in range(depth // chunk):
            hit = key[:, kk * chunk : (kk + 1) * chunk] == target
            perm_v[:, kk * chunk : (kk + 1) * chunk] = jnp.where(hit, 1.0, 0.0).astype(jnp.bfloat16)
        step = min(rows, 256)

        def body(r, carry):
            at_row = pl.multiple_of(r * step, step)
            wp_v[i, pl.ds(at_row, step), :] = lax.dot_general(
                w_v[pl.ds(at_row, step), :], perm_v[...], (((1,), (1,)), ((), ())),
                preferred_element_type=jnp.float32,
            ).astype(jnp.bfloat16)
            return carry

        lax.fori_loop(0, rows // step, body, 0)

    def pass_along(label):
        kind, h = label
        i = at[label]
        if kind == "f" and h < nf:
            n = at[("f", h + 1)]
            start(remote(gz[i], gz[n], z_send.at[n, 0], z_recv.at[n, 0], zfore))
        if kind == "b" and h < nb:
            n = at[("b", h + 1)]
            start(remote(gz[i], gz[n], z_send.at[n, 0], z_recv.at[n, 0], zback))

    def pass_along_hi(label):
        kind, h = label
        i = at[label]
        if kind in "of" and h < nf:
            n = at[("f", h + 1)]
            start(remote(gx[i], gx[n], x_send.at[n, 0], x_recv.at[n, 0], zfore))
        if kind in "ob" and h < nb:
            n = at[("b", h + 1)]
            start(remote(gx[i], gx[n], x_send.at[n, 0], x_recv.at[n, 0], zback))

    def cut(src, height, region, owner, dst):
        lane = lax.broadcasted_iota(jnp.int32, (height, MAX_LAG), 1)
        word = tabs_s[region, 0, owner]
        block = lax.bitwise_and(word, 3)
        lag = lax.shift_right_logical(word, 2)
        turn = lax.bitwise_and(MAX_LAG - lag, MAX_LAG - 1)
        near = lane < MAX_LAG - lag
        held = pltpu.roll(src[block, 0:height, 0:MAX_LAG].astype(jnp.float32), turn, 1)
        for j in range(seg // MAX_LAG):
            following = pltpu.roll(
                src[block, 0:height, (j + 1) * MAX_LAG : (j + 2) * MAX_LAG].astype(jnp.float32), turn, 1
            )
            dst[:, j * MAX_LAG : (j + 1) * MAX_LAG] = jnp.where(near, held, following).astype(jnp.bfloat16)
            held = following

    def owner_at(label, xx):
        return lax.rem(z + zoff(label) + nz, nz) * 2 * NX + col(xx, c)

    def near_tiles(label):
        i = at[label]
        t = tslot(label)
        k = col(x, c)
        owner = owner_at(label, x)
        for j in range(4):
            n = 5 * i + j
            cut(gz[i], BLOCK_CH, 2 + j, owner, full.at[n])
            start(remote(full.at[n], tiles.at[t, k], f_send.at[n], t_recv.at[t, k, 0], peers[1 + j]))
        for j in range(2):
            n = 3 * i + j
            cut(gz[i], HALF, 6 + j, owner, half.at[n])
            start(
                remote(half.at[n], tiles.at[t, k, pl.ds(0, HALF)], h_send.at[n], t_recv.at[t, k, 0], peers[5 + j])
            )
        n = 5 * i + 4
        cut(gz[i], BLOCK_CH, 1, owner, full.at[n])
        start(remote(full.at[n], tiles.at[t, k], f_send.at[n], t_recv.at[t, k, 0], sibling))
        cut(gz[i], BLOCK_CH, 0, owner, tiles.at[t, k])

    def hi_tiles(label):
        i = at[label]
        t = tslot(label)
        k = col(x + 2, c)
        owner = owner_at(label, x + 2)
        n = 3 * i + 2
        cut(gx[i], HALF, 1, owner, half.at[n])
        start(remote(half.at[n], tiles.at[t, k, hi], h_send.at[n], t_recv.at[t, k, 1], sibling))
        cut(gx[i], HALF, 0, owner, tiles.at[t, k, hi])

    def wait_z(label):
        i = at[label]
        if label[1] == 1:
            for part, cols in enumerate((main, rim)):
                dst = gz[i].at[:, :, cols]
                remote(dst, dst, z_send.at[i, part], z_recv.at[i, part], zfore).wait_recv()
        else:
            remote(gz[i], gz[i], z_send.at[i, 0], z_recv.at[i, 0], zfore).wait_recv()

    def wait_hi(label):
        i = at[label]
        if label[1] == 0:
            for part, cols in enumerate((main, rim)):
                dst = gx[i].at[:, :, cols]
                remote(dst, dst, x_send.at[i, part], x_recv.at[i, part], zfore).wait_recv()
        else:
            remote(gx[i], gx[i], x_send.at[i, 0], x_recv.at[i, 0], zfore).wait_recv()

    def wait_tiles(label):
        t = tslot(label)
        for k in (col(x, e), col(x + 1, c), col(x + 1, e), col(x - 1, c), col(x - 1, e)):
            remote(full.at[0], tiles.at[t, k], f_send.at[0], t_recv.at[t, k, 0], sibling).wait_recv()
        for cc in (c, e):
            k = col(x + 2, cc)
            dst = tiles.at[t, k, pl.ds(0, HALF)]
            remote(half.at[0], dst, h_send.at[0], t_recv.at[t, k, 0], sibling).wait_recv()
        k = col(x + 2, e)
        remote(half.at[0], tiles.at[t, k, hi], h_send.at[0], t_recv.at[t, k, 1], sibling).wait_recv()

    width = min(seg, 256)

    def add_chunk(label):
        t = tslot(label)
        i = at[label]
        wait_tiles(label)

        def body(n, carry):
            cols = pl.ds(pl.multiple_of(n * width, width), width)
            part = jnp.dot(
                wp_v[i], tiles[t, :, :, cols].reshape(chunk, width), preferred_element_type=jnp.float32
            )
            acc[n] = part if i == 0 else acc[n] + part
            return carry

        lax.fori_loop(0, seg // width, body, 0)

    w_copy.wait()
    arrange(labels[0])
    if ny > 1:
        @pl.when(y < ny - 1)
        def _():
            halo.wait_recv()
    for n, peer in firsts:
        start(remote(own.at[:, :, rim], gz[n].at[:, :, rim], z_send.at[n, 1], z_recv.at[n, 1], peer))
    start(remote(own.at[:, hi, rim], gx[0].at[:, :, rim], x_send.at[0, 1], x_recv.at[0, 1], opposite))
    for slot, peer in zip(slots, peers):
        remote(tab_v, tabs_v.at[slot], tab_send.at[0], tab_recv.at[slot], peer).wait_recv()
    to_smem = pltpu.make_async_copy(tabs_v, tabs_s, smem_sem)
    to_smem.start()
    to_smem.wait()
    own_copy.wait()
    near_tiles(labels[0])

    by_hop = [[label for label in labels if label[1] == h] for h in range(nf + 1)]
    to_arrange = list(labels[1:])
    to_add = list(labels)
    for h in range(1, nf + 1):
        for label in by_hop[h]:
            wait_z(label)
            pass_along(label)
        for label in by_hop[h]:
            near_tiles(label)
        for label in by_hop[h - 1]:
            wait_hi(label)
            pass_along_hi(label)
            hi_tiles(label)
        for _ in range(2):
            if to_arrange:
                arrange(to_arrange.pop(0))
        if h >= 2:
            for _ in by_hop[h - 2]:
                add_chunk(to_add.pop(0))
    while to_arrange:
        arrange(to_arrange.pop(0))
    while len(to_add) > len(by_hop[nf]):
        add_chunk(to_add.pop(0))
    for label in by_hop[nf]:
        wait_hi(label)
        hi_tiles(label)
        add_chunk(label)

    block = 128
    for r in range(rows // block):
        total = jnp.zeros((block, 128), jnp.float32)
        for n in range(seg // width):
            for j in range(width // 128):
                part = acc[n, r * block : (r + 1) * block, j * 128 : (j + 1) * 128]
                total = total + part * part
        ebuf[y, r : r + 1, :] = jnp.sum(total.T, axis=0, keepdims=True)

    for k, peer in enumerate(others):
        start(remote(ebuf.at[y], ebuf.at[y], y_send.at[k], y_recv.at[y], peer))
    for k in range(1, ny):
        source = lax.rem(y + k, ny)
        remote(ebuf.at[source], ebuf.at[source], y_send.at[0], y_recv.at[source], others[0]).wait_recv()
    energy = ebuf[0]
    for k in range(1, ny):
        energy = energy + ebuf[k]
    log_power = jnp.log(energy / samples + 1e-06)
    per = SRC_BLOCK // block
    for r in range(rows // block):
        lp_ref[r // per : r // per + 1, (r % per) * block : (r % per + 1) * block] = log_power[r : r + 1, :]
    powers = lp_ref[...]
    classes = cw_ref.shape[0]
    place = lax.broadcasted_iota(jnp.int32, (powers.shape[0], classes), 1)
    scores = jnp.broadcast_to(cb_ref[...], place.shape)
    for j in range(classes):
        score = jnp.sum(powers * cw_ref[j : j + 1, :], axis=1, keepdims=True)
        scores = scores + jnp.where(place == j, score, 0.0)
    lg_ref[...] = scores
    for copy in sent:
        copy.wait_send()
    if ny > 1:
        @pl.when(y > 0)
        def _():
            halo.wait_send()


def per_device(nz, ny, traces, stack_weights, channel_lists, lag_offsets, lengths, class_weights, class_bias):
    blocks = traces.shape[0] // BLOCK_CH
    seg = traces.shape[1]
    rows, depth = stack_weights.shape
    chunk = 2 * NX * BLOCK_CH
    bf16, f32 = jnp.bfloat16, jnp.float32
    vmem = pl.BlockSpec(memory_space=pltpu.VMEM)
    hbm = pl.BlockSpec(memory_space=pl.ANY)
    dma = pltpu.SemaphoreType.DMA
    width = min(seg, 256)
    scratch = (
        [pltpu.VMEM((blocks, BLOCK_CH, seg + MAX_LAG), bf16) for _ in range(nz)]
        + [pltpu.VMEM((blocks, HALF, seg + MAX_LAG), bf16) for _ in range(nz)]
        + [
            pltpu.VMEM((nz, 2 * NX, BLOCK_CH, seg), bf16),
            pltpu.VMEM((5 * nz, BLOCK_CH, seg), bf16),
            pltpu.VMEM((3 * nz, HALF, seg), bf16),
            pltpu.VMEM((rows, depth), bf16),
            pltpu.VMEM((chunk, depth), bf16),
            pltpu.VMEM((nz, rows, chunk), bf16),
            pltpu.VMEM((seg // width, rows, width), f32),
            pltpu.VMEM((8, 128), jnp.int32),
            pltpu.VMEM((8, 128), jnp.int32),
            pltpu.VMEM((8, 8, 128), jnp.int32),
            pltpu.SMEM((8, 8, 128), jnp.int32),
            pltpu.VMEM((ny, rows // 128, 128), f32),
            dma((2,)), dma((2,)), dma((7,)), dma((8,)), dma,
            dma((nz, 2)), dma((nz, 2)), dma((nz, 2)), dma((nz, 2)),
            dma((5 * nz,)), dma((3 * nz,)), dma((nz, 2 * NX, 2)), dma((ny,)), dma((ny,)),
        ]
    )
    return pl.pallas_call(
        functools.partial(kernel, nz, ny, float(seg * ny)),
        out_shape=(
            jax.ShapeDtypeStruct((rows // SRC_BLOCK, SRC_BLOCK), f32),
            jax.ShapeDtypeStruct((rows // SRC_BLOCK, class_weights.shape[1]), f32),
        ),
        in_specs=[vmem, vmem, vmem, hbm, hbm, vmem, vmem],
        out_specs=(vmem, vmem),
        scratch_shapes=scratch,
        compiler_params=pltpu.CompilerParams(
            collective_id=0, has_side_effects=True, vmem_limit_bytes=56 * 1024 * 1024
        ),
    )(
        channel_lists, lag_offsets, lengths.reshape(1, 1), traces.reshape(blocks, BLOCK_CH, seg), stack_weights,
        class_weights.T, class_bias.reshape(1, -1),
    )


def solution(mesh):
    placed = (
        P("fibre", "tm"),
        P("fibre", None),
        P("fibre", None),
        P("fibre", None),
        P("fibre"),
        P(),
        P(),
    )
    nz = mesh.shape["fibre"] // (2 * NX)
    return jax.shard_map(
        functools.partial(per_device, nz, mesh.shape["tm"]),
        mesh=mesh,
        in_specs=placed,
        out_specs=(P("fibre", None), P("fibre", None)),
        check_vma=False,
    )
```

time: 104 us -> 74.3 us (0.71)
  Pallas kernels: 96.7 us -> 70.3 us
  local copies, waits for them, and re-layouts: 5.26 us -> 2.5 us
    pallas_call x1, Pallas kernels: 96.7 us -> 70.3 us  [per_device(): pl.pallas_call(functools.partial(kernel, nz, ny, float(seg * ny)), out_sh...]
    unnamed x3 -> x2, local copies, waits for them, and re-layouts: 3.96 us -> 2.5 us
    broadcast_in_dim x2 -> x0, local copies, waits for them, and re-layouts: 1.23 us -> none  [the longest x1 0.63 us: per_device(): key = jnp.broadcast_to(keyed.reshape(1, depth), (8, depth))]
where the time goes in v2:
time: 74.3 us; the launch traced here: 74 us
  Pallas kernels  70.3 us (95%)
  local copies, waits for them, and re-layouts  2.5 us (3%)
  between operations  1.29 us (2%)
    pallas_call x1, Pallas kernels, per_device(): pl.pallas_call(functools.partial(kernel, nz, ny, float(seg * ny)), out_sh...  70.3 us
    unnamed x2, local copies, waits for them, and re-layouts  2.5 us

profile of v2, /device:TPU:1, one launch (start us, length us, event | category | flops | bytes accessed | tf_op | source)
XLA Modules:
  0.0 74.0 jit_solution(16016139727681567930)
XLA Ops:
  1.3 70.3 %shard_map.86 = (f32[4,256]{1,0:T(4,128)}, f32[4,4]{1,0:T(4,128)}) custom-call(s32[1,64]{1,0:T(1,128)} %list_ref.1, s32[1,64]{1,0:T(1,128)} %lag_ref.1, s32[1,1]{1,0:T(1,128)} %bitcast.4.len_ref, bf16[4,32,1024]{2,1,0:T(8,128)(2,1)} %bitcast.5, bf16[1024,2048]{1,0:T(8,128)(2,1)} %w_ref.1, f32[4,256]{1,0:T(4,128)} %bitcast.6, f32[1,4]{1,0:T(1,128)} %bitcast.7), custom_call_target="tpu_custom_call" | custom-call | tf_op jit(solution)/shard_map/pallas_call | solution.py:383
  71.6 1.3 %copy.12 = f32[4,256]{1,0:T(4,128)} copy(f32[4,256]{1,0:T(4,128)} %get-tuple-element.4) | data formatting | bytes 8192
  72.8 1.2 %copy.13 = f32[4,4]{1,0:T(4,128)} copy(f32[4,4]{1,0:T(4,128)} %get-tuple-element.5) | data formatting | bytes 128

commit v3 on v2

v3 whole, which is shorter than its diff:
```python
import functools

import jax
import jax.numpy as jnp
from jax import lax
from jax.experimental import pallas as pl
from jax.experimental.pallas import tpu as pltpu
from jax.sharding import PartitionSpec as P

BLOCK_CH = 32
MAX_LAG = 128
SRC_BLOCK = 256
NX = 4
HALF = BLOCK_CH // 2
EARLY, LATER = 1, 2
MESH = pl.DeviceIdType.MESH


def kernel(
    nz, ny, list_hbm, lag_hbm, len_hbm, traces_ref, w_ref, energy_ref, *scratch
):
    nf = nz // 2
    nb = nz - 1 - nf
    labels = [("o", 0)]
    for h in range(1, nf + 1):
        labels.append(("f", h))
        if h <= nb:
            labels.append(("b", h))
    at = {label: i for i, label in enumerate(labels)}
    gz = scratch[:nz]
    gx = scratch[nz : 2 * nz]
    gs = scratch[2 * nz : 3 * nz]
    gsx = scratch[3 * nz : 4 * nz]
    (
        tiles, full, half, w_v, perm_v, wp_v, acc, squares, list_ref, lag_ref, len_ref, pad, tab_v, tabs_v, tabs_s, ebuf,
        loc_sem, halo_sem, tab_send, tab_recv, smem_sem,
        z_send, z_recv, x_send, x_recv, s_send, s_recv, sx_send, sx_recv, f_send, h_send, t_recv, y_send, y_recv,
    ) = scratch[4 * nz :]
    seg = traces_ref.shape[2]
    rows = w_ref.shape[0]
    depth = w_ref.shape[1]
    count = list_ref.shape[1]
    chunk = 2 * NX * BLOCK_CH

    me = lax.axis_index("fibre")
    y = lax.axis_index("tm")
    c = lax.rem(me, 2)
    x = lax.rem(me // 2, NX)
    z = me // (2 * NX)
    d = 1 - 2 * c
    e = 1 - c

    def dev(zz, xx, cc):
        return {"fibre": (lax.rem(zz + 2 * nz, nz) * NX + lax.rem(xx + 2 * NX, NX)) * 2 + cc}

    def zoff(label):
        kind, h = label
        return {"o": 0, "f": -d * h, "b": d * h}[kind]

    def tslot(label):
        return lax.rem(zoff(label) + nz, nz)

    def col(xx, cc):
        return lax.rem(xx + 2 * NX, NX) * 2 + cc

    sibling = dev(z, x, e)
    peers = [dev(z, x + s, c) for s in (1, -1, 2)]
    slots = [2, 1, 3]
    opposite = peers[2]
    zfore, zback = dev(z + d, x, c), dev(z - d, x, c)
    ring = [zfore, zback] if nb else [zfore]
    others = [{"tm": lax.rem(y + k, ny)} for k in range(1, ny)]

    fetched = [
        pltpu.make_async_copy(src, dst, loc_sem.at[2 + i])
        for i, (src, dst) in enumerate(((list_hbm, list_ref), (lag_hbm, lag_ref), (len_hbm, len_ref)))
    ]
    for copy in fetched:
        copy.start()
    own = gz[0]
    hi = pl.ds(HALF, HALF)
    main, rim = pl.ds(0, seg), pl.ds(seg, MAX_LAG)
    own_copy = pltpu.make_async_copy(traces_ref, own.at[:, :, main], loc_sem.at[0])
    own_copy.start()
    w_copy = pltpu.make_async_copy(w_ref, w_v, loc_sem.at[1])
    w_copy.start()
    barrier = pltpu.get_barrier_semaphore()
    near = [sibling] + peers + ring
    for peer in near + others:
        pl.semaphore_signal(barrier, inc=1, device_id=peer, device_id_type=MESH)
    for copy in fetched:
        copy.wait()
    pad[...] = jnp.zeros_like(pad)
    pad[0:1, 0:count] = list_ref[...] + 256 * lag_ref[...]
    asked = jnp.broadcast_to(pad[0:1, :], (128, 128)).T[0:count, :]
    owner_of = lax.shift_right_logical(lax.bitwise_and(asked, 255), 2)
    word = lax.bitwise_or(
        lax.bitwise_and(asked, 3), lax.shift_left(lax.shift_right_logical(asked, 8), 2)
    )
    wanted = lax.broadcasted_iota(jnp.int32, (count, 128), 1)
    table = jnp.sum(jnp.where(owner_of == wanted, word, 0), axis=0, keepdims=True)
    tab_v[...] = jnp.broadcast_to(table, (8, 128))
    tabs_v[0] = tab_v[...]
    live = lax.broadcasted_iota(jnp.int32, (1, count), 1) < len_ref[...]
    keyed = jnp.where(live, lax.shift_right_logical(list_ref[...], 2), 2 * nz * NX)
    spread = lax.shift_right_logical(lax.broadcasted_iota(jnp.int32, (count, depth), 1), 5)
    spread = spread == lax.broadcasted_iota(jnp.int32, (count, depth), 0)
    key = jnp.dot(
        jnp.broadcast_to(keyed, (8, count)).astype(jnp.float32).astype(jnp.bfloat16),
        jnp.where(spread, 1.0, 0.0).astype(jnp.bfloat16),
        preferred_element_type=jnp.float32,
    )
    inner = lax.bitwise_and(lax.broadcasted_iota(jnp.int32, (1, depth), 1), BLOCK_CH - 1)
    key = key[0:1, :].astype(jnp.int32) * BLOCK_CH + inner

    @pl.when(y == ny - 1)
    def _():
        own[:, :, seg:] = jnp.zeros((own.shape[0], BLOCK_CH, MAX_LAG), jnp.bfloat16)

    pl.semaphore_wait(barrier, len(near) + len(others))

    def remote(src, dst, ssem, rsem, device):
        return pltpu.make_async_remote_copy(
            src_ref=src, dst_ref=dst, send_sem=ssem, recv_sem=rsem, device_id=device, device_id_type=MESH
        )

    sent = []

    def start(copy):
        copy.start()
        sent.append(copy)

    halo = remote(
        traces_ref.at[:, :, pl.ds(0, MAX_LAG)], own.at[:, :, rim],
        halo_sem.at[0], halo_sem.at[1], {"tm": lax.rem(y + ny - 1, ny)},
    )
    if ny > 1:
        @pl.when(y > 0)
        def _():
            halo.start()
    firsts = [(at[("f", 1)], zfore)] + ([(at[("b", 1)], zback)] if nb else [])
    for n, peer in firsts:
        start(remote(traces_ref, gz[n].at[:, :, main], z_send.at[n, 0], z_recv.at[n, 0], peer))
    start(remote(traces_ref.at[:, hi], gx[0].at[:, :, main], x_send.at[0, 0], x_recv.at[0, 0], opposite))
    for i, (slot, peer) in enumerate(zip(slots, peers)):
        start(remote(tab_v, tabs_v.at[slot], tab_send.at[i], tab_recv.at[slot], peer))

    def arrange(label):
        i = at[label]
        first = lax.rem(z + zoff(label) + nz, nz) * chunk
        target = lax.broadcasted_iota(jnp.int32, (chunk, chunk), 0) + first
        for kk in range(depth // chunk):
            hit = key[:, kk * chunk : (kk + 1) * chunk] == target
            perm_v[:, kk * chunk : (kk + 1) * chunk] = jnp.where(hit, 1.0, 0.0).astype(jnp.bfloat16)
        step = min(rows, 256)

        def body(r, carry):
            at_row = pl.multiple_of(r * step, step)
            wp_v[i, pl.ds(at_row, step), :] = lax.dot_general(
                w_v[pl.ds(at_row, step), :], perm_v[...], (((1,), (1,)), ((), ())),
                preferred_element_type=jnp.float32,
            ).astype(jnp.bfloat16)
            return carry

        lax.fori_loop(0, rows // step, body, 0)

    def pass_along(label):
        kind, h = label
        i = at[label]
        if kind == "f" and h < nf:
            n = at[("f", h + 1)]
            start(remote(gz[i], gz[n], z_send.at[n, 0], z_recv.at[n, 0], zfore))
        if kind == "b" and h < nb:
            n = at[("b", h + 1)]
            start(remote(gz[i], gz[n], z_send.at[n, 0], z_recv.at[n, 0], zback))

    def pass_along_hi(label):
        kind, h = label
        i = at[label]
        if kind in "of" and h < nf:
            n = at[("f", h + 1)]
            start(remote(gx[i], gx[n], x_send.at[n, 0], x_recv.at[n, 0], zfore))
        if kind in "ob" and h < nb:
            n = at[("b", h + 1)]
            start(remote(gx[i], gx[n], x_send.at[n, 0], x_recv.at[n, 0], zback))

    def cut(src, height, region, owner, dst):
        lane = lax.broadcasted_iota(jnp.int32, (height, MAX_LAG), 1)
        word = tabs_s[region, 0, owner]
        block = lax.bitwise_and(word, 3)
        lag = lax.shift_right_logical(word, 2)
        turn = lax.bitwise_and(MAX_LAG - lag, MAX_LAG - 1)
        near = lane < MAX_LAG - lag
        held = pltpu.roll(src[block, 0:height, 0:MAX_LAG].astype(jnp.float32), turn, 1)
        for j in range(seg // MAX_LAG):
            following = pltpu.roll(
                src[block, 0:height, (j + 1) * MAX_LAG : (j + 2) * MAX_LAG].astype(jnp.float32), turn, 1
            )
            dst[:, j * MAX_LAG : (j + 1) * MAX_LAG] = jnp.where(near, held, following).astype(jnp.bfloat16)
            held = following

    def mirror(label):
        kind, h = label
        return {"o": ("o", 0), "f": ("b", h) if h <= nb else ("f", h), "b": ("f", h)}[kind]

    def swap(label):
        i = at[label]
        start(remote(gz[i], gs[i], s_send.at[i], s_recv.at[i], sibling))

    def swap_hi(label):
        i = at[label]
        start(remote(gx[i], gsx[i], sx_send.at[i], sx_recv.at[i], sibling))

    def near_tiles(label):
        i = at[label]
        t = tslot(label)
        m = at[mirror(label)]
        remote(gs[m], gs[m], s_send.at[m], s_recv.at[m], sibling).wait_recv()
        first = lax.rem(z + zoff(label) + nz, nz) * 2 * NX + 2 * x
        mine = pl.ds(2 * x, 2)
        for j in range(2):
            n = 2 * i + j
            cut(gz[i], BLOCK_CH, 1 + j, first + c, full.at[n, c])
            cut(gs[m], BLOCK_CH, 1 + j, first + e, full.at[n, e])
            start(remote(full.at[n], tiles.at[t, mine], f_send.at[n], t_recv.at[t, x], peers[j]))
        cut(gz[i], HALF, 3, first + c, half.at[i, c])
        cut(gs[m], HALF, 3, first + e, half.at[i, e])
        start(remote(half.at[i], tiles.at[t, mine, pl.ds(0, HALF)], h_send.at[i], t_recv.at[t, x], opposite))
        cut(gz[i], BLOCK_CH, 0, first + c, tiles.at[t, 2 * x + c])
        cut(gs[m], BLOCK_CH, 0, first + e, tiles.at[t, 2 * x + e])

    def hi_tiles(label):
        i = at[label]
        t = tslot(label)
        m = at[mirror(label)]
        remote(gsx[m], gsx[m], sx_send.at[m], sx_recv.at[m], sibling).wait_recv()
        there = col(x + 2, 0)
        first = lax.rem(z + zoff(label) + nz, nz) * 2 * NX + there
        cut(gx[i], HALF, 0, first + c, tiles.at[t, there + c, hi])
        cut(gsx[m], HALF, 0, first + e, tiles.at[t, there + e, hi])

    def wait_z(label):
        i = at[label]
        if label[1] == 1:
            for part, cols in enumerate((main, rim)):
                dst = gz[i].at[:, :, cols]
                remote(dst, dst, z_send.at[i, part], z_recv.at[i, part], zfore).wait_recv()
        else:
            remote(gz[i], gz[i], z_send.at[i, 0], z_recv.at[i, 0], zfore).wait_recv()

    def wait_hi(label):
        i = at[label]
        if label[1] == 0:
            for part, cols in enumerate((main, rim)):
                dst = gx[i].at[:, :, cols]
                remote(dst, dst, x_send.at[i, part], x_recv.at[i, part], zfore).wait_recv()
        else:
            remote(gx[i], gx[i], x_send.at[i, 0], x_recv.at[i, 0], zfore).wait_recv()

    def wait_tiles(label):
        t = tslot(label)
        for step in (1, -1):
            source = lax.rem(x + step + NX, NX)
            dst = tiles.at[t, pl.ds(2 * source, 2)]
            remote(full.at[0], dst, f_send.at[0], t_recv.at[t, source], sibling).wait_recv()
        source = lax.rem(x + 2, NX)
        dst = tiles.at[t, pl.ds(2 * source, 2), pl.ds(0, HALF)]
        remote(half.at[0], dst, h_send.at[0], t_recv.at[t, source], sibling).wait_recv()

    width = min(seg, 256)

    def add_chunk(label):
        t = tslot(label)
        i = at[label]
        wait_tiles(label)

        def body(n, carry):
            cols = pl.ds(pl.multiple_of(n * width, width), width)
            part = jnp.dot(
                wp_v[i], tiles[t, :, :, cols].reshape(chunk, width), preferred_element_type=jnp.float32
            )
            if i > 0:
                part = acc[n] + part
            if i < nz - 1:
                acc[n] = part
            else:
                part = part * part
                square = part[:, 0:128]
                for j in range(1, width // 128):
                    square = square + part[:, j * 128 : (j + 1) * 128]
                squares[...] = squares[...] + square
            return carry

        if i == nz - 1:
            squares[...] = jnp.zeros_like(squares)

        lax.fori_loop(0, seg // width, body, 0)

    to_arrange = list(labels)
    to_add = list(labels)

    def work(arranges, adds):
        for _ in range(arranges):
            if to_arrange:
                arrange(to_arrange.pop(0))
        for _ in range(adds):
            while len(to_arrange) >= len(to_add):
                arrange(to_arrange.pop(0))
            add_chunk(to_add.pop(0))

    own_copy.wait()
    if ny > 1:
        @pl.when(y < ny - 1)
        def _():
            halo.wait_recv()
    for n, peer in firsts:
        start(remote(own.at[:, :, rim], gz[n].at[:, :, rim], z_send.at[n, 1], z_recv.at[n, 1], peer))
    start(remote(own.at[:, hi, rim], gx[0].at[:, :, rim], x_send.at[0, 1], x_recv.at[0, 1], opposite))
    swap(labels[0])
    w_copy.wait()
    work(EARLY, 0)
    for slot, peer in zip(slots, peers):
        remote(tab_v, tabs_v.at[slot], tab_send.at[0], tab_recv.at[slot], peer).wait_recv()
    to_smem = pltpu.make_async_copy(tabs_v, tabs_s, smem_sem)
    to_smem.start()
    to_smem.wait()
    near_tiles(labels[0])
    work(LATER, 0)

    by_hop = [[label for label in labels if label[1] == h] for h in range(nf + 1)]
    for h in range(1, nf + 1):
        for label in by_hop[h]:
            wait_z(label)
            pass_along(label)
            swap(label)
        if h < 3:
            work(1, 0)
        else:
            work(0, 1)
        for label in by_hop[h]:
            near_tiles(label)
        if h < 3:
            work(1, 0)
        else:
            work(0, 1)
        for label in by_hop[h - 1]:
            wait_hi(label)
            pass_along_hi(label)
            swap_hi(label)
        if h == 1:
            work(1, 0)
        if h == 2:
            work(0, 1)
        for label in by_hop[h - 1]:
            hi_tiles(label)
    for label in by_hop[nf]:
        wait_hi(label)
        swap_hi(label)
    while len(to_add) > len(by_hop[nf]):
        work(0, 1)
    for label in by_hop[nf]:
        hi_tiles(label)
        work(0, 1)

    block = 128
    for r in range(rows // block):
        part = squares[r * block : (r + 1) * block, :]
        ebuf[y, r : r + 1, :] = jnp.sum(part.T, axis=0, keepdims=True)

    for k, peer in enumerate(others):
        start(remote(ebuf.at[y], ebuf.at[y], y_send.at[k], y_recv.at[y], peer))
    for k in range(1, ny):
        source = lax.rem(y + k, ny)
        remote(ebuf.at[source], ebuf.at[source], y_send.at[0], y_recv.at[source], others[0]).wait_recv()
    energy = ebuf[0]
    for k in range(1, ny):
        energy = energy + ebuf[k]
    energy_ref[...] = energy
    for copy in sent:
        copy.wait_send()
    if ny > 1:
        @pl.when(y > 0)
        def _():
            halo.wait_send()


def classify(samples, energy_ref, cw_ref, cb_ref, lp_ref, lg_ref):
    log_power = jnp.log(energy_ref[...] / samples + 1e-06)
    per = SRC_BLOCK // 128
    for r in range(log_power.shape[0]):
        lp_ref[r // per : r // per + 1, (r % per) * 128 : (r % per + 1) * 128] = log_power[r : r + 1, :]
    powers = lp_ref[...]
    classes = cw_ref.shape[0]
    place = lax.broadcasted_iota(jnp.int32, (powers.shape[0], classes), 1)
    scores = jnp.broadcast_to(cb_ref[...], place.shape)
    for j in range(classes):
        score = jnp.sum(powers * cw_ref[j : j + 1, :], axis=1, keepdims=True)
        scores = scores + jnp.where(place == j, score, 0.0)
    lg_ref[...] = scores


def per_device(nz, ny, traces, stack_weights, channel_lists, lag_offsets, lengths, class_weights, class_bias):
    blocks = traces.shape[0] // BLOCK_CH
    seg = traces.shape[1]
    rows, depth = stack_weights.shape
    chunk = 2 * NX * BLOCK_CH
    bf16, f32 = jnp.bfloat16, jnp.float32
    vmem = pl.BlockSpec(memory_space=pltpu.VMEM)
    hbm = pl.BlockSpec(memory_space=pl.ANY)
    dma = pltpu.SemaphoreType.DMA
    width = min(seg, 256)
    whole = pltpu.VMEM((blocks, BLOCK_CH, seg + MAX_LAG), bf16)
    upper = pltpu.VMEM((blocks, HALF, seg + MAX_LAG), bf16)
    scratch = (
        [whole] * nz
        + [upper] * nz
        + [whole] * nz
        + [upper] * nz
        + [
            pltpu.VMEM((nz, 2 * NX, BLOCK_CH, seg), bf16),
            pltpu.VMEM((2 * nz, 2, BLOCK_CH, seg), bf16),
            pltpu.VMEM((nz, 2, HALF, seg), bf16),
            pltpu.VMEM((rows, depth), bf16),
            pltpu.VMEM((chunk, depth), bf16),
            pltpu.VMEM((nz, rows, chunk), bf16),
            pltpu.VMEM((seg // width, rows, width), f32),
            pltpu.VMEM((rows, 128), f32),
            pltpu.VMEM(channel_lists.shape, jnp.int32),
            pltpu.VMEM(channel_lists.shape, jnp.int32),
            pltpu.VMEM((1, 1), jnp.int32),
            pltpu.VMEM((8, 128), jnp.int32),
            pltpu.VMEM((8, 128), jnp.int32),
            pltpu.VMEM((4, 8, 128), jnp.int32),
            pltpu.SMEM((4, 8, 128), jnp.int32),
            pltpu.VMEM((ny, rows // 128, 128), f32),
            dma((5,)), dma((2,)), dma((3,)), dma((4,)), dma,
            dma((nz, 2)), dma((nz, 2)), dma((nz, 2)), dma((nz, 2)),
            dma((nz,)), dma((nz,)), dma((nz,)), dma((nz,)),
            dma((2 * nz,)), dma((nz,)), dma((nz, NX)), dma((ny,)), dma((ny,)),
        ]
    )
    energy = pl.pallas_call(
        functools.partial(kernel, nz, ny),
        out_shape=jax.ShapeDtypeStruct((rows // 128, 128), f32),
        in_specs=[hbm] * 5,
        out_specs=vmem,
        scratch_shapes=scratch,
        compiler_params=pltpu.CompilerParams(
            collective_id=0, has_side_effects=True, vmem_limit_bytes=56 * 1024 * 1024
        ),
    )(channel_lists, lag_offsets, lengths.reshape(1, 1), traces.reshape(blocks, BLOCK_CH, seg), stack_weights)
    return pl.pallas_call(
        functools.partial(classify, float(seg * ny)),
        out_shape=(
            jax.ShapeDtypeStruct((rows // SRC_BLOCK, SRC_BLOCK), f32),
            jax.ShapeDtypeStruct((rows // SRC_BLOCK, class_weights.shape[1]), f32),
        ),
        in_specs=[vmem] * 3,
        out_specs=(vmem, vmem),
    )(energy, class_weights.T, class_bias.reshape(1, -1))


def solution(mesh):
    placed = (
        P("fibre", "tm"),
        P("fibre", None),
        P("fibre", None),
        P("fibre", None),
        P("fibre"),
        P(),
        P(),
    )
    nz = mesh.shape["fibre"] // (2 * NX)
    return jax.shard_map(
        functools.partial(per_device, nz, mesh.shape["tm"]),
        mesh=mesh,
        in_specs=placed,
        out_specs=(P("fibre", None), P("fibre", None)),
        check_vma=False,
    )
```

time: 74.3 us -> 71.7 us (0.965)
  local copies, waits for them, and re-layouts: 2.5 us -> 0 us
    unnamed x2 -> x0, local copies, waits for them, and re-layouts: 2.5 us -> none
    pallas_call x1 -> x2, Pallas kernels: 70.3 us -> 70.2 us  [the longest x1 68.8 us: per_device(): pl.pallas_call(functools.partial(kernel, nz, ny), out_shape=jax.ShapeDtyp...]
where the time goes in v3:
time: 71.7 us; the launch traced here: 71.5 us
  Pallas kernels  70.2 us (98%)
  between operations  1.29 us (2%)
    pallas_call x1, Pallas kernels, per_device(): pl.pallas_call(functools.partial(kernel, nz, ny), out_shape=jax.ShapeDtyp...  68.8 us

profile of v3, /device:TPU:1, one launch (start us, length us, event | category | flops | bytes accessed | tf_op | source)
XLA Modules:
  0.0 71.5 jit_solution(16944838709898809401)
XLA Ops:
  1.3 68.8 %shard_map.86.energy_ref = f32[8,128]{1,0:T(8,128)} custom-call(s32[1,64]{1,0:T(1,128)} %list_hbm.1, s32[1,64]{1,0:T(1,128)} %lag_hbm.1, s32[1,1]{1,0:T(1,128)} %bitcast.4.len_hbm, bf16[4,32,1024]{2,1,0:T(8,128)(2,1)} %bitcast.5, bf16[1024,2048]{1,0:T(8,128)(2,1)} %w_ref.1), custom_call_target="tpu_custom_call" | custom-call | tf_op jit(solution)/shard_map/pallas_call | solution.py:442
  70.1 1.4 %shard_map.87 = (f32[4,256]{1,0:T(4,128)}, f32[4,4]{1,0:T(4,128)}) custom-call(f32[8,128]{1,0:T(8,128)} %shard_map.86.energy_ref, f32[4,256]{1,0:T(4,128)} %bitcast.6, f32[1,4]{1,0:T(1,128)} %bitcast.7), custom_call_target="tpu_custom_call" | custom-call | tf_op jit(solution)/shard_map/pallas_call | solution.py:452

commit v4 on v3

--- a/solution.py
+++ b/solution.py
@@ -152,7 +152,7 @@
         for kk in range(depth // chunk):
             hit = key[:, kk * chunk : (kk + 1) * chunk] == target
             perm_v[:, kk * chunk : (kk + 1) * chunk] = jnp.where(hit, 1.0, 0.0).astype(jnp.bfloat16)
-        step = min(rows, 256)
+        step = min(rows, 1024)
 
         def body(r, carry):
             at_row = pl.multiple_of(r * step, step)
@@ -269,17 +269,21 @@
 
     width = min(seg, 256)
 
-    def add_chunk(label):
-        t = tslot(label)
-        i = at[label]
-        wait_tiles(label)
+    def add_chunk(*group):
+        i = at[group[-1]]
+        for label in group:
+            wait_tiles(label)
 
         def body(n, carry):
             cols = pl.ds(pl.multiple_of(n * width, width), width)
-            part = jnp.dot(
-                wp_v[i], tiles[t, :, :, cols].reshape(chunk, width), preferred_element_type=jnp.float32
+            part = sum(
+                jnp.dot(
+                    wp_v[at[label]], tiles[tslot(label), :, :, cols].reshape(chunk, width),
+                    preferred_element_type=jnp.float32,
+                )
+                for label in group
             )
-            if i > 0:
+            if at[group[0]] > 0:
                 part = acc[n] + part
             if i < nz - 1:
                 acc[n] = part
@@ -303,10 +307,11 @@
         for _ in range(arranges):
             if to_arrange:
                 arrange(to_arrange.pop(0))
-        for _ in range(adds):
-            while len(to_arrange) >= len(to_add):
-                arrange(to_arrange.pop(0))
-            add_chunk(to_add.pop(0))
+        group = [to_add.pop(0) for _ in range(adds)]
+        while group and len(to_arrange) > len(to_add):
+            arrange(to_arrange.pop(0))
+        if group:
+            add_chunk(*group)
 
     own_copy.wait()
     if ny > 1:
@@ -333,16 +338,14 @@
             wait_z(label)
             pass_along(label)
             swap(label)
-        if h < 3:
+        if h <= 2:
             work(1, 0)
-        else:
-            work(0, 1)
         for label in by_hop[h]:
             near_tiles(label)
-        if h < 3:
+        if h <= 2:
             work(1, 0)
-        else:
-            work(0, 1)
+        if h > 2:
+            work(0, len(by_hop[h - 2]))
         for label in by_hop[h - 1]:
             wait_hi(label)
             pass_along_hi(label)
@@ -357,7 +360,7 @@
         wait_hi(label)
         swap_hi(label)
     while len(to_add) > len(by_hop[nf]):
-        work(0, 1)
+        work(0, min(2, len(to_add) - len(by_hop[nf])))
     for label in by_hop[nf]:
         hi_tiles(label)
         work(0, 1)

time: 71.7 us -> 68.3 us (0.953)
  Pallas kernels: 70.2 us -> 66.8 us
    pallas_call x1, Pallas kernels: 68.8 us -> 65.4 us  [per_device(): pl.pallas_call(functools.partial(kernel, nz, ny), out_shape=jax.ShapeDtyp...]
where the time goes in v4:
time: 68.3 us; the launch traced here: 68.1 us
  Pallas kernels  66.8 us (98%)
  between operations  1.29 us (2%)
    pallas_call x1, Pallas kernels, per_device(): pl.pallas_call(functools.partial(kernel, nz, ny), out_shape=jax.ShapeDtyp...  65.4 us
    pallas_call x1, Pallas kernels, per_device(): pl.pallas_call(functools.partial(classify, float(seg * ny)), out_shape=(j...  1.4 us

profile of v4, /device:TPU:1, one launch (start us, length us, event | category | flops | bytes accessed | tf_op | source)
XLA Modules:
  0.0 68.1 jit_solution(6482837140476990406)
XLA Ops:
  1.3 65.4 %shard_map.86.energy_ref = f32[8,128]{1,0:T(8,128)} custom-call(s32[1,64]{1,0:T(1,128)} %list_hbm.1, s32[1,64]{1,0:T(1,128)} %lag_hbm.1, s32[1,1]{1,0:T(1,128)} %bitcast.4.len_hbm, bf16[4,32,1024]{2,1,0:T(8,128)(2,1)} %bitcast.5, bf16[1024,2048]{1,0:T(8,128)(2,1)} %w_ref.1), custom_call_target="tpu_custom_call" | custom-call | tf_op jit(solution)/shard_map/pallas_call | solution.py:445
  66.7 1.4 %shard_map.87 = (f32[4,256]{1,0:T(4,128)}, f32[4,4]{1,0:T(4,128)}) custom-call(f32[8,128]{1,0:T(8,128)} %shard_map.86.energy_ref, f32[4,256]{1,0:T(4,128)} %bitcast.6, f32[1,4]{1,0:T(1,128)} %bitcast.7), custom_call_target="tpu_custom_call" | custom-call | tf_op jit(solution)/shard_map/pallas_call | solution.py:455

commit v5 on v4

--- a/solution.py
+++ b/solution.py
@@ -69,7 +69,8 @@
     opposite = peers[2]
     zfore, zback = dev(z + d, x, c), dev(z - d, x, c)
     ring = [zfore, zback] if nb else [zfore]
-    others = [{"tm": lax.rem(y + k, ny)} for k in range(1, ny)]
+    far_first = sorted(range(1, ny), key=lambda k: -min(k, ny - k))
+    others = [{"tm": lax.rem(y + k, ny)} for k in far_first]
 
     fetched = [
         pltpu.make_async_copy(src, dst, loc_sem.at[2 + i])

time: 68.3 us -> 68.1 us (level)
  no operation moved by 1% of the time
where the time goes in v5:
time: 68.1 us; the launch traced here: 68 us
  Pallas kernels  66.7 us (98%)
  between operations  1.29 us (2%)
    pallas_call x1, Pallas kernels, per_device(): pl.pallas_call(functools.partial(kernel, nz, ny), out_shape=jax.ShapeDtyp...  65.3 us
    pallas_call x1, Pallas kernels, per_device(): pl.pallas_call(functools.partial(classify, float(seg * ny)), out_shape=(j...  1.4 us

profile of v5, /device:TPU:1, one launch (start us, length us, event | category | flops | bytes accessed | tf_op | source)
XLA Modules:
  0.0 68.0 jit_solution(10507605379868224691)
XLA Ops:
  1.3 65.3 %shard_map.86.energy_ref = f32[8,128]{1,0:T(8,128)} custom-call(s32[1,64]{1,0:T(1,128)} %list_hbm.1, s32[1,64]{1,0:T(1,128)} %lag_hbm.1, s32[1,1]{1,0:T(1,128)} %bitcast.4.len_hbm, bf16[4,32,1024]{2,1,0:T(8,128)(2,1)} %bitcast.5, bf16[1024,2048]{1,0:T(8,128)(2,1)} %w_ref.1), custom_call_target="tpu_custom_call" | custom-call | tf_op jit(solution)/shard_map/pallas_call | solution.py:446
  66.6 1.4 %shard_map.87 = (f32[4,256]{1,0:T(4,128)}, f32[4,4]{1,0:T(4,128)}) custom-call(f32[8,128]{1,0:T(8,128)} %shard_map.86.energy_ref, f32[4,256]{1,0:T(4,128)} %bitcast.6, f32[1,4]{1,0:T(1,128)} %bitcast.7), custom_call_target="tpu_custom_call" | custom-call | tf_op jit(solution)/shard_map/pallas_call | solution.py:456
